TPU v7x, 32 devices: a whole 2x2x4 slice. The times are simulated.
32 devices in a mesh: fsdp: 2 (over x), ctx: 4 (over y, core), tp: 4 (over z).
Axes of the slice: x: 2, y: 2, z: 4, core: 2. Of those that a mesh axis runs over, the one named last changes fastest.
Arguments:
- tokens: bfloat16 [2, 2048, 2304], P('fsdp', 'ctx'), may hold values from -6 to 6
- q_weight: bfloat16 [2304, 2048], P(('fsdp', 'ctx'), 'tp'), as said below
- key_weight: bfloat16 [2304, 1024], P(('fsdp', 'ctx'), 'tp'), may hold values from -0.125 to 0.125
- value_weight: bfloat16 [2304, 1024], P(('fsdp', 'ctx'), 'tp'), may hold values from -0.125 to 0.125
- out_weight: bfloat16 [2048, 2304], P('tp', ('fsdp', 'ctx')), may hold values from -0.125 to 0.125
- gate_weight: bfloat16 [2304, 9216], P(('fsdp', 'ctx'), 'tp'), may hold values from -0.125 to 0.125
- up_weight: bfloat16 [2304, 9216], P(('fsdp', 'ctx'), 'tp'), may hold values from -0.125 to 0.125
- down_weight: bfloat16 [9216, 2304], P('tp', ('fsdp', 'ctx')), may hold values from -0.0625 to 0.0625
- gain_attn_in: bfloat16 [2304], P(('fsdp', 'ctx')), may hold values from 0.099609375 to 1.8984375
- gain_attn_out: bfloat16 [2304], P(('fsdp', 'ctx')), may hold values from 0.099609375 to 1.8984375
- gain_mlp_in: bfloat16 [2304], P(('fsdp', 'ctx')), may hold values from 0.099609375 to 1.8984375
- gain_mlp_out: bfloat16 [2304], P(('fsdp', 'ctx')), may hold values from 0.099609375 to 1.8984375
- segment_ids: int32 [2, 2048], P('fsdp'), may hold values from 0 to 4, as said below
- block_order: int32 [2, 8], P('fsdp'), may hold values from 0 to 7, as said below
- cotangent: bfloat16 [2, 2048, 2304], P('fsdp', 'ctx'), may hold values from -6 to 6
Outputs:
- layer_out: bfloat16 [2, 2048, 2304], P('fsdp', 'ctx')
- grad_tokens: float32 [2, 2048, 2304], P('fsdp', 'ctx')
- grad_q_weight: float32 [2304, 2048], P(('fsdp', 'ctx'), 'tp')
- grad_key_weight: float32 [2304, 1024], P(('fsdp', 'ctx'), 'tp')
- grad_value_weight: float32 [2304, 1024], P(('fsdp', 'ctx'), 'tp')
- grad_out_weight: float32 [2048, 2304], P('tp', ('fsdp', 'ctx'))
- grad_gate_weight: float32 [2304, 9216], P(('fsdp', 'ctx'), 'tp')
- grad_up_weight: float32 [2304, 9216], P(('fsdp', 'ctx'), 'tp')
- grad_down_weight: float32 [9216, 2304], P('tp', ('fsdp', 'ctx'))
- grad_gain_attn_in: float32 [2304], P(('fsdp', 'ctx'))
- grad_gain_attn_out: float32 [2304], P(('fsdp', 'ctx'))
- grad_gain_mlp_in: float32 [2304], P(('fsdp', 'ctx'))
- grad_gain_mlp_out: float32 [2304], P(('fsdp', 'ctx'))
Inputs may be any that keep to these rules, and one draw needn't show every extreme that they name: `segment_ids`: along each sequence the ids never fall; every one of the 5 documents is present; document 0 covers at least the first 1024 positions. `block_order`: each row is a permutation of the 8 blocks; stored blocks 2j and 2j + 1 hold true blocks b and 7 - b for some b. `q_weight`: every entry is at most 24 / sqrt(2304) in magnitude.
All inputs are finite; a program needn't handle non-finite values.
Results may differ from a plain program's by a relative error of at most 0.023.
The roundings to bfloat16 on the way count: a program that leaves them out, or rounds other values in their place, can miss the bound.
Values may be sent and summed in bfloat16 or wider, within the bound.
No kernel may reach another device: no remote copies, remote signals or barrier semaphores. Data moves between devices by JAX's collectives and lax.ppermute only.
A program may use at most 256 MiB of HBM per device.

v0:
```python
import jax
import jax.numpy as jnp
from jax import lax
from jax.sharding import PartitionSpec as P

HEAD_DIM = 256
BLOCK = 256
EPS = 1e-06
CAP = 50.0
THETA = 10000.0


def normalize(values, gain):
    return (
        values
        * lax.rsqrt(jnp.mean(values * values, axis=-1, keepdims=True) + EPS)
        * gain.astype(jnp.float32)
    )


def normalize_back(values, gain, upstream):
    inverse = lax.rsqrt(jnp.mean(values * values, axis=-1, keepdims=True) + EPS)
    scaled = upstream * gain.astype(jnp.float32)
    d_values = inverse * scaled - values * inverse * inverse * inverse * jnp.mean(
        scaled * values, axis=-1, keepdims=True
    )
    d_gain = jnp.sum(upstream * values * inverse, axis=0)
    return (d_values, d_gain)


def angles_for(positions, width):
    half = width // 2
    freqs = THETA ** (-jnp.arange(half, dtype=jnp.float32) * 2.0 / width)
    angles = positions.astype(jnp.float32)[:, None] * freqs[None, :]
    return (jnp.cos(angles)[:, None, :], jnp.sin(angles)[:, None, :], half)


def rotate(values, positions):
    cosine, sine, half = angles_for(positions, values.shape[-1])
    first = values[..., :half]
    second = values[..., half:]
    return jnp.concatenate(
        [first * cosine - second * sine, second * cosine + first * sine], axis=-1
    )


def rotate_back(grads, positions):
    cosine, sine, half = angles_for(positions, grads.shape[-1])
    first = grads[..., :half]
    second = grads[..., half:]
    return jnp.concatenate(
        [first * cosine + second * sine, second * cosine - first * sine], axis=-1
    )


def outer(left, right):
    return lax.dot_general(
        left, right, (((0,), (0,)), ((), ())), preferred_element_type=jnp.float32
    )


def times_transposed(left, right):
    return lax.dot_general(
        left, right, (((1,), (1,)), ((), ())), preferred_element_type=jnp.float32
    )


def masked_scores(query_block, pos_block, seg_block, keys_all, key_pos, key_seg):
    scores = jnp.einsum("rd,kd->rk", query_block, keys_all, preferred_element_type=jnp.float32)
    bent = jnp.tanh(scores / CAP)
    allowed = (seg_block[:, None] == key_seg[None, :]) & (
        (pos_block // BLOCK)[:, None] >= (key_pos // BLOCK)[None, :]
    )
    return (jnp.where(allowed, CAP * bent, -1e30), bent)


def per_device(
    tokens,
    q_weight,
    key_weight,
    value_weight,
    out_weight,
    gate_weight,
    up_weight,
    down_weight,
    gain_attn_in,
    gain_attn_out,
    gain_mlp_in,
    gain_mlp_out,
    segment_ids,
    block_order,
    cotangent,
):
    inputs = tokens[0].astype(jnp.float32)
    tok_count = inputs.shape[0]
    q_full, key_full, value_full, out_full, gain_one, gain_two = (
        lax.all_gather(q_weight, ("fsdp", "ctx"), axis=0, tiled=True),
        lax.all_gather(key_weight, ("fsdp", "ctx"), axis=0, tiled=True),
        lax.all_gather(value_weight, ("fsdp", "ctx"), axis=0, tiled=True),
        lax.all_gather(out_weight, ("fsdp", "ctx"), axis=1, tiled=True),
        lax.all_gather(gain_attn_in, ("fsdp", "ctx"), axis=0, tiled=True),
        lax.all_gather(gain_attn_out, ("fsdp", "ctx"), axis=0, tiled=True),
    )
    order = block_order[0]
    within = jnp.arange(BLOCK, dtype=jnp.int32)
    key_pos = (order[:, None] * BLOCK + within[None, :]).reshape(-1)
    key_seg = segment_ids[0].reshape(-1, BLOCK)[order].reshape(-1)
    start = lax.axis_index("ctx") * tok_count
    query_pos = lax.dynamic_slice_in_dim(key_pos, start, tok_count)
    query_seg = lax.dynamic_slice_in_dim(key_seg, start, tok_count)
    normed_attn = normalize(inputs, gain_one).astype(jnp.bfloat16)
    q_lin = jnp.dot(normed_attn, q_full, preferred_element_type=jnp.float32)
    heads_local = q_lin.shape[1] // HEAD_DIM
    scale = HEAD_DIM ** (-0.5)
    queries = (rotate(q_lin.reshape(tok_count, heads_local, HEAD_DIM), query_pos) * scale).astype(
        jnp.bfloat16
    )
    key_lin = jnp.dot(normed_attn, key_full, preferred_element_type=jnp.float32)
    keys_own = rotate(key_lin[:, None, :], query_pos)[:, 0, :].astype(jnp.bfloat16)
    values_own = jnp.dot(normed_attn, value_full, preferred_element_type=jnp.float32).astype(
        jnp.bfloat16
    )
    keys_all, values_all = (
        lax.all_gather(keys_own, "ctx", axis=0, tiled=True),
        lax.all_gather(values_own, "ctx", axis=0, tiled=True),
    )
    rows = min(512, tok_count)
    blocks = tok_count // rows
    query_items = queries.transpose(1, 0, 2)
    pos_items = jnp.tile(query_pos.reshape(blocks, rows), (heads_local, 1))
    seg_items = jnp.tile(query_seg.reshape(blocks, rows), (heads_local, 1))

    def forward_item(item):
        query_block, pos_block, seg_block = item
        masked, bent = masked_scores(query_block, pos_block, seg_block, keys_all, key_pos, key_seg)
        highest = jnp.max(masked, axis=-1, keepdims=True)
        expo = jnp.exp(masked - highest)
        total = jnp.sum(expo, axis=-1, keepdims=True)
        weights = (expo / total).astype(jnp.bfloat16)
        output = jnp.einsum("rk,kd->rd", weights, values_all, preferred_element_type=jnp.float32)
        return (output, (highest + jnp.log(total))[:, 0])

    outputs, logsums = lax.map(forward_item, (query_items, pos_items, seg_items))
    attended = (
        outputs.transpose(1, 0, 2).reshape(tok_count, heads_local * HEAD_DIM).astype(jnp.bfloat16)
    )
    branch_attn = lax.psum(jnp.dot(attended, out_full, preferred_element_type=jnp.float32), "tp")
    resid = inputs + normalize(branch_attn, gain_two)
    gate_full, up_full, down_full, gain_three, gain_four = (
        lax.all_gather(gate_weight, ("fsdp", "ctx"), axis=0, tiled=True),
        lax.all_gather(up_weight, ("fsdp", "ctx"), axis=0, tiled=True),
        lax.all_gather(down_weight, ("fsdp", "ctx"), axis=1, tiled=True),
        lax.all_gather(gain_mlp_in, ("fsdp", "ctx"), axis=0, tiled=True),
        lax.all_gather(gain_mlp_out, ("fsdp", "ctx"), axis=0, tiled=True),
    )
    normed_mlp = normalize(resid, gain_three).astype(jnp.bfloat16)
    gate_lin = jnp.dot(normed_mlp, gate_full, preferred_element_type=jnp.float32)
    up_lin = jnp.dot(normed_mlp, up_full, preferred_element_type=jnp.float32)
    activ = (jax.nn.gelu(gate_lin, approximate=True) * up_lin).astype(jnp.bfloat16)
    branch_mlp = lax.psum(jnp.dot(activ, down_full, preferred_element_type=jnp.float32), "tp")
    layer_out = resid + normalize(branch_mlp, gain_four)
    upstream = cotangent[0].astype(jnp.float32)
    d_branch_mlp, grad_gain_four = normalize_back(branch_mlp, gain_four, upstream)
    d_mlp_low = d_branch_mlp.astype(jnp.bfloat16)
    grad_down = outer(activ, d_mlp_low)
    d_activ = times_transposed(d_mlp_low, down_full)
    unused_value, gelu_pullback = jax.vjp(
        lambda gate_in, up_in: jax.nn.gelu(gate_in, approximate=True) * up_in, gate_lin, up_lin
    )
    d_gate, d_up = gelu_pullback(d_activ)
    d_gate_low = d_gate.astype(jnp.bfloat16)
    d_up_low = d_up.astype(jnp.bfloat16)
    grad_gate = outer(normed_mlp, d_gate_low)
    grad_up = outer(normed_mlp, d_up_low)
    d_normed_mlp = lax.psum(
        times_transposed(d_gate_low, gate_full) + times_transposed(d_up_low, up_full), "tp"
    )
    d_resid_mlp, grad_gain_three = normalize_back(resid, gain_three, d_normed_mlp)
    d_resid = upstream + d_resid_mlp
    d_branch_attn, grad_gain_two = normalize_back(branch_attn, gain_two, d_resid)
    d_attn_low = d_branch_attn.astype(jnp.bfloat16)
    grad_out = outer(attended, d_attn_low)
    d_attended = times_transposed(d_attn_low, out_full).astype(jnp.bfloat16)
    d_items = d_attended.reshape(tok_count, heads_local, HEAD_DIM).transpose(1, 0, 2)

    def backward_item(sums, item):
        query_block, pos_block, seg_block, d_out, logsum = item
        masked, bent = masked_scores(query_block, pos_block, seg_block, keys_all, key_pos, key_seg)
        probs = jnp.exp(masked - logsum[:, None])
        weights = probs.astype(jnp.bfloat16)
        d_weights = jnp.einsum("rd,kd->rk", d_out, values_all, preferred_element_type=jnp.float32)
        d_values_sum = sums[1] + jnp.einsum(
            "rk,rd->kd", weights, d_out, preferred_element_type=jnp.float32
        )
        inner = jnp.sum(probs * d_weights, axis=-1, keepdims=True)
        d_scores = (probs * (d_weights - inner) * (1.0 - bent * bent)).astype(jnp.bfloat16)
        d_query = jnp.einsum("rk,kd->rd", d_scores, keys_all, preferred_element_type=jnp.float32)
        d_keys_sum = sums[0] + jnp.einsum(
            "rk,rd->kd", d_scores, query_block, preferred_element_type=jnp.float32
        )
        return ((d_keys_sum, d_values_sum), d_query)

    zeros_kv = jnp.zeros(keys_all.shape, jnp.float32)
    (d_keys_every, d_values_every), d_query_items = lax.scan(
        backward_item, (zeros_kv, zeros_kv), (query_items, pos_items, seg_items, d_items, logsums)
    )
    d_keys_rot, d_values_mine = (
        lax.psum_scatter(d_keys_every, "ctx", scatter_dimension=0, tiled=True),
        lax.psum_scatter(d_values_every, "ctx", scatter_dimension=0, tiled=True),
    )
    d_key_lin = rotate_back(d_keys_rot[:, None, :], query_pos)[:, 0, :].astype(jnp.bfloat16)
    d_value_lin = d_values_mine.astype(jnp.bfloat16)
    d_queries = d_query_items.transpose(1, 0, 2)
    d_q_lin = (
        rotate_back(d_queries * scale, query_pos)
        .reshape(tok_count, heads_local * HEAD_DIM)
        .astype(jnp.bfloat16)
    )
    grad_query = outer(normed_attn, d_q_lin)
    grad_key = outer(normed_attn, d_key_lin)
    grad_value = outer(normed_attn, d_value_lin)
    d_normed_attn = lax.psum(
        (
            times_transposed(d_q_lin, q_full)
            + times_transposed(d_key_lin, key_full)
            + times_transposed(d_value_lin, value_full)
        ).astype(jnp.bfloat16),
        "tp",
    ).astype(jnp.float32)
    d_tokens_attn, grad_gain_one = normalize_back(inputs, gain_one, d_normed_attn)
    grad_tokens = d_resid + d_tokens_attn
    every_grad = (
        lax.psum_scatter(
            grad_query.astype(jnp.bfloat16), ("fsdp", "ctx"), scatter_dimension=0, tiled=True
        ).astype(jnp.float32),
        lax.psum_scatter(
            grad_key.astype(jnp.bfloat16), ("fsdp", "ctx"), scatter_dimension=0, tiled=True
        ).astype(jnp.float32),
        lax.psum_scatter(
            grad_value.astype(jnp.bfloat16), ("fsdp", "ctx"), scatter_dimension=0, tiled=True
        ).astype(jnp.float32),
        lax.psum_scatter(
            grad_out.astype(jnp.bfloat16), ("fsdp", "ctx"), scatter_dimension=1, tiled=True
        ).astype(jnp.float32),
        lax.psum_scatter(
            grad_gain_one.astype(jnp.bfloat16), ("fsdp", "ctx"), scatter_dimension=0, tiled=True
        ).astype(jnp.float32),
        lax.psum_scatter(
            grad_gain_two.astype(jnp.bfloat16), ("fsdp", "ctx"), scatter_dimension=0, tiled=True
        ).astype(jnp.float32),
        lax.psum_scatter(
            grad_gate.astype(jnp.bfloat16), ("fsdp", "ctx"), scatter_dimension=0, tiled=True
        ).astype(jnp.float32),
        lax.psum_scatter(
            grad_up.astype(jnp.bfloat16), ("fsdp", "ctx"), scatter_dimension=0, tiled=True
        ).astype(jnp.float32),
        lax.psum_scatter(
            grad_down.astype(jnp.bfloat16), ("fsdp", "ctx"), scatter_dimension=1, tiled=True
        ).astype(jnp.float32),
        lax.psum_scatter(
            grad_gain_three.astype(jnp.bfloat16), ("fsdp", "ctx"), scatter_dimension=0, tiled=True
        ).astype(jnp.float32),
        lax.psum_scatter(
            grad_gain_four.astype(jnp.bfloat16), ("fsdp", "ctx"), scatter_dimension=0, tiled=True
        ).astype(jnp.float32),
    )
    attn_results = every_grad[:6]
    mlp_results = every_grad[6:]
    return (
        layer_out.astype(jnp.bfloat16)[None],
        grad_tokens[None],
        attn_results[0],
        attn_results[1],
        attn_results[2],
        attn_results[3],
        mlp_results[0],
        mlp_results[1],
        mlp_results[2],
        attn_results[4],
        attn_results[5],
        mlp_results[3],
        mlp_results[4],
    )


def solution(mesh):
    return jax.shard_map(
        per_device,
        mesh=mesh,
        in_specs=(
            P("fsdp", "ctx", None),
            P(("fsdp", "ctx"), "tp"),
            P(("fsdp", "ctx"), "tp"),
            P(("fsdp", "ctx"), "tp"),
            P("tp", ("fsdp", "ctx")),
            P(("fsdp", "ctx"), "tp"),
            P(("fsdp", "ctx"), "tp"),
            P("tp", ("fsdp", "ctx")),
            P(("fsdp", "ctx")),
            P(("fsdp", "ctx")),
            P(("fsdp", "ctx")),
            P(("fsdp", "ctx")),
            P("fsdp", None),
            P("fsdp", None),
            P("fsdp", "ctx", None),
        ),
        out_specs=(
            P("fsdp", "ctx", None),
            P("fsdp", "ctx", None),
            P(("fsdp", "ctx"), "tp"),
            P(("fsdp", "ctx"), "tp"),
            P(("fsdp", "ctx"), "tp"),
            P("tp", ("fsdp", "ctx")),
            P(("fsdp", "ctx"), "tp"),
            P(("fsdp", "ctx"), "tp"),
            P("tp", ("fsdp", "ctx")),
            P(("fsdp", "ctx")),
            P(("fsdp", "ctx")),
            P(("fsdp", "ctx")),
            P(("fsdp", "ctx")),
        ),
        check_vma=False,
    )
```

profile of v0, /device:TPU:0, one launch (start us, length us, event | category | flops | bytes accessed | tf_op | source)
XLA Modules:
  0.0 1594.3 jit_solution(6297504366629576011)
XLA Ops:
  14.2 25.8 %all-reduce.9 = (bf16[2304]{0:T(1024)(128)(2,1)S(1)}, bf16[2304]{0:T(1024)(128)(2,1)S(1)}, bf16[2304]{0:T(1024)(128)(2,1)S(1)}, bf16[2304]{0:T(1024)(128)(2,1)S(1)}) all-reduce(bf16[2304]{0:T(1024)(128)(2,1)S(1)} %dynamic-update-slice, bf16[2304]{0:T(1024)(128)(2,1)S(1)} %dynamic-update-slice.1, ...), channel_id=1, replica_groups=mesh['fsdp'=2,'ctx'=4,'tp'=4] {'fsdp','ctx'}, use_global_device_ids=true, to_apply=%add | all-reduce | flops 9216 | bytes 36864
  48.9 14.0 all-gather.15.cloned.1.call-done
  70.9 10.9 all-gather.27.cloned.1.call-done
  83.3 29.3 %all-gather.11.cloned.1.call-done = bf16[2304,512]{1,0:T(8,128)(2,1)} async-done(((bf16[288,512]{1,0:T(8,128)(2,1)}), bf16[2304,512]{1,0:T(8,128)(2,1)}) %all-gather.11.cloned.1.call-update) | async-done | bytes 2359312 | tf_op jit(solution)/shard_map/all_gather | solution.py:97
  131.3 20.2 %while.39 = (s32[]{:T(128)}, bf16[2,512,256]{1,2,0:T(8,128)(2,1)}, f32[2,512]{1,0:T(2,128)S(1)}, s32[2,512]{1,0:T(2,128)S(1)}, s32[8,256]{1,0:T(8,128)S(1)}, /*i...) while((s32[]{:T(128)}, bf16[2,512,256]{1,2,0:T(8,128)(2,1)}, ...), condition=%wide.region_4.5_spmd.clone.clone.clone, body=%wide.region_1.4_spmd.clone.clone.sunk.clone | while | flops 1086364672 | bytes 32425128 | solution.py:143
  151.5 10.6 all-gather.19.cloned.1.call-done
  169.8 169.9 %all-reduce.15.cloned.1.call-done = f32[512,2304]{1,0:T(8,128)} async-done(((f32[512,2304]{1,0:T(8,128)}), f32[512,2304]{1,0:T(8,128)}) %all-reduce.15.cloned.1.call-update) | async-done | bytes 4718608 | tf_op jit(solution)/shard_map/psum | solution.py:147
  347.2 57.2 %all-gather.21.cloned.1.call-done = bf16[2304,2304]{1,0:T(8,128)(2,1)} async-done(((bf16[288,2304]{1,0:T(8,128)(2,1)}), bf16[2304,2304]{1,0:T(8,128)(2,1)}) %all-gather.21.cloned.1.call-update) | async-done | bytes 10616848 | tf_op jit(solution)/shard_map/all_gather | solution.py:150
  404.5 11.3 fusion.125
  415.7 54.5 %all-gather.23.cloned.1.call-done = bf16[2304,2304]{1,0:T(8,128)(2,1)} async-done(((bf16[288,2304]{1,0:T(8,128)(2,1)}), bf16[2304,2304]{1,0:T(8,128)(2,1)}) %all-gather.23.cloned.1.call-update) | async-done | bytes 10616848 | tf_op jit(solution)/shard_map/all_gather | solution.py:151
  470.2 12.5 multiply_convert_fusion.2
  482.7 53.1 %all-gather.25.cloned.1.call-done = bf16[2304,2304]{0,1:T(8,128)(2,1)} async-done(((bf16[2304,288]{0,1:T(8,128)(2,1)}), bf16[2304,2304]{0,1:T(8,128)(2,1)}) %all-gather.25.cloned.1.call-update) | async-done | bytes 10616848 | tf_op jit(solution)/shard_map/all_gather | solution.py:152
  535.8 11.7 fusion.126
  547.7 171.9 %all-reduce.17.cloned.1.call-done = f32[512,2304]{1,0:T(8,128)} async-done(((f32[512,2304]{1,0:T(8,128)}), f32[512,2304]{1,0:T(8,128)}) %all-reduce.17.cloned.1.call-update) | async-done | bytes 4718608 | tf_op jit(solution)/shard_map/psum | solution.py:160
  730.7 14.7 multiply_convert_fusion.1
  745.5 9.5 fusion.127
  754.9 12.2 convolution_add_fusion.4
  767.6 170.6 %all-reduce.19.cloned.1.call-done = f32[512,2304]{1,0:T(8,128)} async-done(((f32[512,2304]{1,0:T(8,128)}), f32[512,2304]{1,0:T(8,128)}) %all-reduce.19.cloned.1.call-update) | async-done | bytes 4718608 | tf_op jit(solution)/shard_map/psum | solution.py:175
  955.8 34.3 %while.40 = (s32[]{:T(128)}, f32[2048,256]{1,0:T(8,128)}, f32[2048,256]{1,0:T(8,128)}, f32[2,512,256]{1,2,0:T(8,128)}, s32[2,512]{1,0:T(2,128)S(1)}, /*index=5*/...) while((s32[]{:T(128)}, f32[2048,256]{1,0:T(8,128)}, ...), condition=%wide.region_16.17_spmd.clone.clone.clone.clone, body=%wide.region_14.16_spmd.clone.clone.clone.sunk.clone | while | flops 2717948928 | bytes 95113088 | solution.py:204
  1003.6 20.0 %reduce-scatter.10.cloned.1.call-done = f32[512,256]{0,1:T(8,128)} async-done(((f32[2048,256]{0,1:T(8,128)}), f32[512,256]{0,1:T(8,128)}) %reduce-scatter.10.cloned.1.call-update) | async-done | bytes 524304 | tf_op jit(solution)/shard_map/reduce_scatter | solution.py:208
  1028.0 29.6 %reduce-scatter.12.cloned.1.call-done = f32[512,256]{1,0:T(8,128)} async-done(((f32[2048,256]{1,0:T(8,128)}), f32[512,256]{1,0:T(8,128)}) %reduce-scatter.12.cloned.1.call-update) | async-done | bytes 524304 | tf_op jit(solution)/shard_map/reduce_scatter | solution.py:209
  1066.8 10.6 convolution_convert_fusion
  1077.5 10.3 convolution_convert_fusion.2
  1087.8 10.6 convolution_convert_fusion.1
  1105.1 44.2 %reduce-scatter.20.cloned.1.call-done = bf16[512,288]{0,1:T(8,128)(2,1)} async-done(((bf16[512,2304]{0,1:T(8,128)(2,1)}), bf16[512,288]{0,1:T(8,128)(2,1)}) %reduce-scatter.20.cloned.1.call-update) | async-done | bytes 294928 | tf_op jit(solution)/shard_map/reduce_scatter | solution.py:242
  1151.2 38.0 %reduce-scatter.16.cloned.1.call-done = bf16[288,256]{1,0:T(8,128)(2,1)} async-done(((bf16[2304,256]{1,0:T(8,128)(2,1)}), bf16[288,256]{1,0:T(8,128)(2,1)}) %reduce-scatter.16.cloned.1.call-update) | async-done | bytes 147472 | tf_op jit(solution)/shard_map/reduce_scatter | solution.py:236
  1190.8 38.6 %reduce-scatter.18.cloned.1.call-done = bf16[288,256]{1,0:T(8,128)(2,1)} async-done(((bf16[2304,256]{1,0:T(8,128)(2,1)}), bf16[288,256]{1,0:T(8,128)(2,1)}) %reduce-scatter.18.cloned.1.call-update) | async-done | bytes 147472 | tf_op jit(solution)/shard_map/reduce_scatter | solution.py:239
  1231.1 96.9 %all-reduce.21.cloned.1.call-done = bf16[512,2304]{1,0:T(8,128)(2,1)} async-done(((bf16[512,2304]{1,0:T(8,128)(2,1)}), bf16[512,2304]{1,0:T(8,128)(2,1)}) %all-reduce.21.cloned.1.call-update) | async-done | bytes 2359312 | tf_op jit(solution)/shard_map/psum | solution.py:222
  1331.5 24.0 %all-reduce.8 = (bf16[2304]{0:T(1024)(128)(2,1)S(1)}, bf16[2304]{0:T(1024)(128)(2,1)S(1)}, bf16[2304]{0:T(1024)(128)(2,1)S(1)}, bf16[2304]{0:T(1024)(128)(2,1)S(1)}) all-reduce(bf16[2304]{0:T(1024)(128)(2,1)S(1)} %get-tuple-element.658, ...), channel_id=12, replica_groups=mesh['fsdp'=2,'ctx'=4,'tp'=4] {'fsdp','ctx'}, use_global_device_ids=true, to_apply=%region_29.30.clone | all-reduce | flops 9216 | bytes 36864
  1364.3 48.4 %reduce-scatter.26.cloned.1.call-done = bf16[2304,288]{0,1:T(8,128)(2,1)} async-done(((bf16[2304,2304]{0,1:T(8,128)(2,1)}), bf16[2304,288]{0,1:T(8,128)(2,1)}) %reduce-scatter.26.cloned.1.call-update) | async-done | bytes 1327120 | tf_op jit(solution)/shard_map/reduce_scatter | solution.py:257
  1415.7 82.8 %reduce-scatter.22.cloned.1.call-done = bf16[288,2304]{1,0:T(8,128)(2,1)} async-done(((bf16[2304,2304]{1,0:T(8,128)(2,1)}), bf16[288,2304]{1,0:T(8,128)(2,1)}) %reduce-scatter.22.cloned.1.call-update) | async-done | bytes 1327120 | tf_op jit(solution)/shard_map/reduce_scatter | solution.py:251
  1501.5 82.8 %reduce-scatter.24.cloned.1.call-done = bf16[288,2304]{1,0:T(8,128)(2,1)} async-done(((bf16[2304,2304]{1,0:T(8,128)(2,1)}), bf16[288,2304]{1,0:T(8,128)(2,1)}) %reduce-scatter.24.cloned.1.call-update) | async-done | bytes 1327120 | tf_op jit(solution)/shard_map/reduce_scatter | solution.py:254
  (330 shorter events, 200.8 us)
Async XLA Ops:
  7.2 36.0 %all-gather.13.cloned.1.call-start = ((), (), s32[]{:S(2)}) async-start(), calls=%async_computation.10 | async-start | bytes 1327104 | tf_op jit(solution)/shard_map/all_gather | solution.py:98
  7.9 55.0 %all-gather.15.cloned.1.call-start = ((), (), s32[]{:S(2)}) async-start(), calls=%async_computation.11 | async-start | bytes 1327104 | tf_op jit(solution)/shard_map/all_gather | solution.py:99
  8.7 73.1 %all-gather.27.cloned.1.call-start = ((), (), s32[]{:S(2)}) async-start(), calls=%async_computation.30 | async-start | bytes 1310720 | tf_op jit(solution)/shard_map/all_gather | solution.py:124
  40.0 76.8 %copy-start.31 = (f32[2304]{0:T(1024)}, f32[2304]{0:T(1024)S(1)}, u32[]{:S(2)}) copy-start(f32[2304]{0:T(1024)S(1)} %convert_element_type.212) | copy-start | bytes 27652
  40.8 25.6 %copy-start.45 = (f32[128]{0:T(128)}, f32[128]{0:T(128)S(1)}, u32[]{:S(2)}) copy-start(f32[128]{0:T(128)S(1)} %multiply_power_fusion) | copy-start | bytes 1540
  40.9 25.5 %copy-start.35 = (f32[512]{0:T(512)}, f32[512]{0:T(512)S(1)}, u32[]{:S(2)}) copy-start(f32[512]{0:T(512)S(1)} %get-tuple-element.717) | copy-start | bytes 6148
  43.1 73.8 %copy-start.42 = (f32[512]{0:T(512)}, f32[512]{0:T(512)S(1)}, u32[]{:S(2)}) copy-start(f32[512]{0:T(512)S(1)} %add_rsqrt_fusion.3) | copy-start | bytes 6148
  48.2 64.4 %all-gather.11.cloned.1.call-start = ((), (), s32[]{:S(2)}) async-start(), calls=%async_computation.9 | async-start | bytes 2654208 | tf_op jit(solution)/shard_map/all_gather | solution.py:97
  48.8 82.5 %all-gather.17.cloned.1.call-start = ((), (), s32[]{:S(2)}) async-start(), calls=%async_computation.12 | async-start | bytes 1310720 | tf_op jit(solution)/shard_map/all_gather | solution.py:125
  65.7 96.4 %all-gather.19.cloned.1.call-start = ((), (), s32[]{:S(2)}) async-start(), calls=%async_computation.13 | async-start | bytes 2654208 | tf_op jit(solution)/shard_map/all_gather | solution.py:100
  66.3 273.4 %all-reduce.15.cloned.1.call-start = ((), (), s32[]{:S(2)}) async-start(), calls=%async_computation.14 | async-start | bytes 9437184 | tf_op jit(solution)/shard_map/psum | solution.py:147
  167.7 236.8 %all-gather.21.cloned.1.call-start = ((), (), s32[]{:S(2)}) async-start(), calls=%async_computation.15 | async-start | bytes 11943936 | tf_op jit(solution)/shard_map/all_gather | solution.py:150
  168.4 301.8 %all-gather.23.cloned.1.call-start = ((), (), s32[]{:S(2)}) async-start(), calls=%async_computation.16 | async-start | bytes 11943936 | tf_op jit(solution)/shard_map/all_gather | solution.py:151
  169.1 366.6 %all-gather.25.cloned.1.call-start = ((), (), s32[]{:S(2)}) async-start(), calls=%async_computation.17 | async-start | bytes 11943936 | tf_op jit(solution)/shard_map/all_gather | solution.py:152
  169.7 549.8 %all-reduce.17.cloned.1.call-start = ((), (), s32[]{:S(2)}) async-start(), calls=%async_computation.18 | async-start | bytes 9437184 | tf_op jit(solution)/shard_map/psum | solution.py:160
  347.2 123.0 %copy-start.17 = (bf16[512,2304]{1,0:T(8,128)(2,1)}, bf16[512,2304]{1,0:T(8,128)(2,1)S(1)}, u32[]{:S(2)}) copy-start(bf16[512,2304]{1,0:T(8,128)(2,1)S(1)} %multiply_convert_fusion.3) | copy-start | bytes 7077892
  547.4 175.0 %copy-start.9 = (bf16[1,512,2304]{2,1,0:T(8,128)(2,1)S(1)}, bf16[1,512,2304]{2,1,0:T(8,128)(2,1)}, u32[]{:S(2)}) copy-start(bf16[1,512,2304]{2,1,0:T(8,128)(2,1)} %param.33) | copy-start | bytes 7077892
  547.5 390.8 %all-reduce.19.cloned.1.call-start = ((), (), s32[]{:S(2)}) async-start(), calls=%async_computation.19 | async-start | bytes 9437184 | tf_op jit(solution)/shard_map/psum | solution.py:175
  767.2 256.4 %reduce-scatter.10.cloned.1.call-start = ((), (), s32[]{:S(2)}) async-start(), calls=%async_computation.20 | async-start | bytes 2621440 | tf_op jit(solution)/shard_map/reduce_scatter | solution.py:208
  993.0 64.5 %reduce-scatter.12.cloned.1.call-start = ((), (), s32[]{:S(2)}) async-start(), calls=%async_computation.21 | async-start | bytes 2621440 | tf_op jit(solution)/shard_map/reduce_scatter | solution.py:209
  993.6 109.7 %reduce-scatter.14.cloned.1.call-start = ((), (), s32[]{:S(2)}) async-start(), calls=%async_computation.23 | async-start | bytes 2654208 | tf_op jit(solution)/shard_map/reduce_scatter | solution.py:233
  998.6 25.0 %copy-start.36 = (f32[512]{0:T(512)S(1)}, f32[512]{0:T(512)}, u32[]{:S(2)}) copy-start(f32[512]{0:T(512)} %copy-done.35) | copy-start | bytes 6148
  998.6 150.7 %reduce-scatter.20.cloned.1.call-start = ((), (), s32[]{:S(2)}) async-start(), calls=%async_computation.26 | async-start | bytes 2654208 | tf_op jit(solution)/shard_map/reduce_scatter | solution.py:242
  1003.5 185.7 %reduce-scatter.16.cloned.1.call-start = ((), (), s32[]{:S(2)}) async-start(), calls=%async_computation.24 | async-start | bytes 1327104 | tf_op jit(solution)/shard_map/reduce_scatter | solution.py:236
  1027.9 201.5 %reduce-scatter.18.cloned.1.call-start = ((), (), s32[]{:S(2)}) async-start(), calls=%async_computation.25 | async-start | bytes 1327104 | tf_op jit(solution)/shard_map/reduce_scatter | solution.py:239
  1060.7 267.4 %all-reduce.21.cloned.1.call-start = ((), (), s32[]{:S(2)}) async-start(), calls=%async_computation.22 | async-start | bytes 4718592 | tf_op jit(solution)/shard_map/psum | solution.py:222
  1066.7 346.0 %reduce-scatter.26.cloned.1.call-start = ((), (), s32[]{:S(2)}) async-start(), calls=%async_computation.29 | async-start | bytes 11943936 | tf_op jit(solution)/shard_map/reduce_scatter | solution.py:257
  1077.4 421.0 %reduce-scatter.22.cloned.1.call-start = ((), (), s32[]{:S(2)}) async-start(), calls=%async_computation.27 | async-start | bytes 11943936 | tf_op jit(solution)/shard_map/reduce_scatter | solution.py:251
  1087.8 496.4 %reduce-scatter.24.cloned.1.call-start = ((), (), s32[]{:S(2)}) async-start(), calls=%async_computation.28 | async-start | bytes 11943936 | tf_op jit(solution)/shard_map/reduce_scatter | solution.py:254
  1098.5 233.0 %copy-start.39 = (bf16[2304]{0:T(1024)(128)(2,1)S(1)}, bf16[2304]{0:T(1024)(128)(2,1)}, u32[]{:S(2)}) copy-start(bf16[2304]{0:T(1024)(128)(2,1)} %get-tuple-element.654) | copy-start | bytes 13828
  1098.5 233.0 %copy-start.40 = (bf16[2304]{0:T(1024)(128)(2,1)S(1)}, bf16[2304]{0:T(1024)(128)(2,1)}, u32[]{:S(2)}) copy-start(bf16[2304]{0:T(1024)(128)(2,1)} %get-tuple-element.656) | copy-start | bytes 13828
  1098.5 233.0 %copy-start.41 = (bf16[2304]{0:T(1024)(128)(2,1)S(1)}, bf16[2304]{0:T(1024)(128)(2,1)}, u32[]{:S(2)}) copy-start(bf16[2304]{0:T(1024)(128)(2,1)} %get-tuple-element.652) | copy-start | bytes 13828
  (56 other events, 368.6 us)
Sparse Core Ops, SparseCore 0:
  9.9 26.9 all-gather.12
  38.7 24.1 all-gather.14
  65.1 16.7 all-gather.26
  83.5 29.0 all-gather.10
  114.6 16.7 all-gather.16
  133.1 29.0 all-gather.18
  167.7 171.9 all-reduce.14
  341.6 62.7 all-gather.20
  406.3 63.8 all-gather.22
  471.9 63.8 all-gather.24
  547.6 171.9 all-reduce.16
  767.3 170.9 all-reduce.18
  993.1 30.4 reduce-scatter.9
  1026.1 31.3 reduce-scatter.11
  1060.7 42.4 reduce-scatter.13
  1106.8 42.4 reduce-scatter.19
  1152.4 36.7 reduce-scatter.15
  1192.6 36.7 reduce-scatter.17
  1232.4 95.5 all-reduce.20
  1331.4 81.2 reduce-scatter.25
  1416.2 82.2 reduce-scatter.21
  1502.0 82.1 reduce-scatter.23
where the time goes:
time: 1600 us; the launch traced here: 1590 us
  waiting for transfers between devices  1240 us (78%)
  matrix products  179 us (11%)
  other arithmetic  77.3 us (5%)
  blocking collectives  49.8 us (3%)
  local copies, waits for them, and re-layouts  29.6 us (2%)
  between operations  16.7 us (1%)
    psum x1, waiting for transfers between devices, per_device(): lax.psum(jnp.dot(activ, down_full, preferred_element_type=jnp.float32), '...  172 us
    psum x1, waiting for transfers between devices, per_device(): lax.psum(times_transposed(d_gate_low, gate_full) + times_transposed(d_up_...  171 us
    psum x1, waiting for transfers between devices, per_device(): lax.psum(jnp.dot(attended, out_full, preferred_element_type=jnp.float32),...  170 us
    psum x1, waiting for transfers between devices, per_device(): lax.psum((times_transposed(d_q_lin, q_full) + times_transposed(d_key_lin,...  96.9 us
    reduce_scatter x1, waiting for transfers between devices, per_device(): lax.psum_scatter(grad_gate.astype(jnp.bfloat16), ('fsdp', 'ctx'), scatter...  82.8 us
    reduce_scatter x1, waiting for transfers between devices, per_device(): lax.psum_scatter(grad_up.astype(jnp.bfloat16), ('fsdp', 'ctx'), scatter_d...  82.8 us
    all_gather x1, waiting for transfers between devices, per_device(): lax.all_gather(gate_weight, ('fsdp', 'ctx'), axis=0, tiled=True)  57.2 us
    all_gather x1, waiting for transfers between devices, per_device(): lax.all_gather(up_weight, ('fsdp', 'ctx'), axis=0, tiled=True)  54.5 us
  transfers between devices with their start and end apart: 22, of which 21 were waited for; matrix products, arithmetic and copies ran while one was open for 10% of the time, Pallas kernels for 0%

commit v1 on v0

--- a/solution.py
+++ b/solution.py
@@ -144,7 +144,9 @@
     attended = (
         outputs.transpose(1, 0, 2).reshape(tok_count, heads_local * HEAD_DIM).astype(jnp.bfloat16)
     )
-    branch_attn = lax.psum(jnp.dot(attended, out_full, preferred_element_type=jnp.float32), "tp")
+    part = jnp.dot(attended, out_full, preferred_element_type=jnp.float32)
+    terms = lax.all_gather(part, "tp", axis=0, tiled=False)
+    branch_attn = terms.sum(axis=0)
     resid = inputs + normalize(branch_attn, gain_two)
     gate_full, up_full, down_full, gain_three, gain_four = (
         lax.all_gather(gate_weight, ("fsdp", "ctx"), axis=0, tiled=True),

time: 1600 us -> 1760 us (1.10)
  waiting for transfers between devices: 1240 us -> 1380 us
    all_gather x0 -> x1, waiting for transfers between devices: none -> 321 us  [per_device(): terms = lax.all_gather(part, 'tp', axis=0, tiled=False)]
    psum x1 -> x0, waiting for transfers between devices: 170 us -> none  [per_device(): lax.psum(jnp.dot(attended, out_full, preferred_element_type=jnp.float32),...]
where the time goes in v1:
time: 1760 us; the launch traced here: 1750 us
  waiting for transfers between devices  1380 us (78%)
  matrix products  178 us (10%)
  other arithmetic  87.7 us (5%)
  blocking collectives  49.8 us (3%)
  local copies, waits for them, and re-layouts  30.1 us (2%)
    all_gather x1, waiting for transfers between devices, per_device(): terms = lax.all_gather(part, 'tp', axis=0, tiled=False)  321 us
    psum x1, waiting for transfers between devices, per_device(): lax.psum(jnp.dot(activ, down_full, preferred_element_type=jnp.float32), '...  172 us
    psum x1, waiting for transfers between devices, per_device(): lax.psum(times_transposed(d_gate_low, gate_full) + times_transposed(d_up_...  171 us
    psum x1, waiting for transfers between devices, per_device(): lax.psum((times_transposed(d_q_lin, q_full) + times_transposed(d_key_lin,...  96.9 us
    reduce_scatter x1, waiting for transfers between devices, per_device(): lax.psum_scatter(grad_gate.astype(jnp.bfloat16), ('fsdp', 'ctx'), scatter...  82.8 us
    reduce_scatter x1, waiting for transfers between devices, per_device(): lax.psum_scatter(grad_up.astype(jnp.bfloat16), ('fsdp', 'ctx'), scatter_d...  82.8 us
    all_gather x1, waiting for transfers between devices, per_device(): lax.all_gather(up_weight, ('fsdp', 'ctx'), axis=0, tiled=True)  54.5 us
    all_gather x1, waiting for transfers between devices, per_device(): lax.all_gather(down_weight, ('fsdp', 'ctx'), axis=1, tiled=True)  53.1 us
  transfers between devices with their start and end apart: 22, of which 21 were waited for; matrix products, arithmetic and copies ran while one was open for 10% of the time, Pallas kernels for 0%

profile of v1, /device:TPU:0, one launch (start us, length us, event | category | flops | bytes accessed | tf_op | source)
XLA Modules:
  0.0 1746.1 jit_solution(7621023788022729259)
XLA Ops:
  14.2 25.8 %all-reduce.9 = (bf16[2304]{0:T(1024)(128)(2,1)S(1)}, bf16[2304]{0:T(1024)(128)(2,1)S(1)}, bf16[2304]{0:T(1024)(128)(2,1)S(1)}, bf16[2304]{0:T(1024)(128)(2,1)S(1)}) all-reduce(bf16[2304]{0:T(1024)(128)(2,1)S(1)} %dynamic-update-slice, bf16[2304]{0:T(1024)(128)(2,1)S(1)} %dynamic-update-slice.1, ...), channel_id=1, replica_groups=mesh['fsdp'=2,'ctx'=4,'tp'=4] {'fsdp','ctx'}, use_global_device_ids=true, to_apply=%add | all-reduce | flops 9216 | bytes 36864
  48.9 14.0 all-gather.17.cloned.1.call-done
  70.9 10.9 all-gather.29.cloned.1.call-done
  83.3 29.3 %all-gather.13.cloned.1.call-done = bf16[2304,512]{1,0:T(8,128)(2,1)} async-done(((bf16[288,512]{1,0:T(8,128)(2,1)}), bf16[2304,512]{1,0:T(8,128)(2,1)}) %all-gather.13.cloned.1.call-update) | async-done | bytes 2359312 | tf_op jit(solution)/shard_map/all_gather | solution.py:97
  131.3 20.2 %while.39 = (s32[]{:T(128)}, bf16[2,512,256]{1,2,0:T(8,128)(2,1)}, f32[2,512]{1,0:T(2,128)S(1)}, s32[2,512]{1,0:T(2,128)S(1)}, s32[8,256]{1,0:T(8,128)S(1)}, /*i...) while((s32[]{:T(128)}, bf16[2,512,256]{1,2,0:T(8,128)(2,1)}, ...), condition=%wide.region_4.5_spmd.clone.clone.clone, body=%wide.region_1.4_spmd.clone.clone.sunk.clone | while | flops 1086364672 | bytes 32425128 | solution.py:143
  151.5 10.6 all-gather.21.cloned.1.call-done
  169.8 320.5 %all-gather.31.cloned.1.call-done = f32[2048,2304]{1,0:T(8,128)} async-done(((f32[512,2304]{1,0:T(8,128)}), f32[2048,2304]{1,0:T(8,128)}) %all-gather.31.cloned.1.call-update) | async-done | bytes 18874384 | tf_op jit(solution)/shard_map/all_gather | solution.py:148
  490.4 10.3 reduce_sum.160
  508.4 46.6 %all-gather.23.cloned.1.call-done = bf16[2304,2304]{1,0:T(8,128)(2,1)} async-done(((bf16[288,2304]{1,0:T(8,128)(2,1)}), bf16[2304,2304]{1,0:T(8,128)(2,1)}) %all-gather.23.cloned.1.call-update) | async-done | bytes 10616848 | tf_op jit(solution)/shard_map/all_gather | solution.py:152
  554.9 11.2 fusion.125
  566.2 54.5 %all-gather.25.cloned.1.call-done = bf16[2304,2304]{1,0:T(8,128)(2,1)} async-done(((bf16[288,2304]{1,0:T(8,128)(2,1)}), bf16[2304,2304]{1,0:T(8,128)(2,1)}) %all-gather.25.cloned.1.call-update) | async-done | bytes 10616848 | tf_op jit(solution)/shard_map/all_gather | solution.py:153
  620.7 12.5 multiply_convert_fusion.2
  633.2 53.1 %all-gather.27.cloned.1.call-done = bf16[2304,2304]{0,1:T(8,128)(2,1)} async-done(((bf16[2304,288]{0,1:T(8,128)(2,1)}), bf16[2304,2304]{0,1:T(8,128)(2,1)}) %all-gather.27.cloned.1.call-update) | async-done | bytes 10616848 | tf_op jit(solution)/shard_map/all_gather | solution.py:154
  686.3 11.7 fusion.126
  698.4 171.6 %all-reduce.14.cloned.1.call-done = f32[512,2304]{1,0:T(8,128)} async-done(((f32[512,2304]{1,0:T(8,128)}), f32[512,2304]{1,0:T(8,128)}) %all-reduce.14.cloned.1.call-update) | async-done | bytes 4718608 | tf_op jit(solution)/shard_map/psum | solution.py:162
  881.2 14.7 multiply_convert_fusion.1
  905.4 12.2 convolution_add_fusion.4
  917.7 171.0 %all-reduce.16.cloned.1.call-done = f32[512,2304]{1,0:T(8,128)} async-done(((f32[512,2304]{1,0:T(8,128)}), f32[512,2304]{1,0:T(8,128)}) %all-reduce.16.cloned.1.call-update) | async-done | bytes 4718608 | tf_op jit(solution)/shard_map/psum | solution.py:177
  1106.6 34.5 %while.40 = (s32[]{:T(128)}, f32[2048,256]{1,0:T(8,128)}, f32[2048,256]{1,0:T(8,128)}, f32[2,512,256]{1,2,0:T(8,128)}, s32[2,512]{1,0:T(2,128)S(1)}, /*index=5*/...) while((s32[]{:T(128)}, f32[2048,256]{1,0:T(8,128)}, ...), condition=%wide.region_16.17_spmd.clone.clone.clone.clone, body=%wide.region_14.16_spmd.clone.clone.clone.sunk.clone | while | flops 2717948928 | bytes 95113088 | solution.py:206
  1154.6 20.0 %reduce-scatter.10.cloned.1.call-done = f32[512,256]{0,1:T(8,128)} async-done(((f32[2048,256]{0,1:T(8,128)}), f32[512,256]{0,1:T(8,128)}) %reduce-scatter.10.cloned.1.call-update) | async-done | bytes 524304 | tf_op jit(solution)/shard_map/reduce_scatter | solution.py:210
  1179.0 29.6 %reduce-scatter.12.cloned.1.call-done = f32[512,256]{1,0:T(8,128)} async-done(((f32[2048,256]{1,0:T(8,128)}), f32[512,256]{1,0:T(8,128)}) %reduce-scatter.12.cloned.1.call-update) | async-done | bytes 524304 | tf_op jit(solution)/shard_map/reduce_scatter | solution.py:211
  1217.8 10.5 convolution_convert_fusion
  1228.4 10.3 convolution_convert_fusion.2
  1238.8 10.6 convolution_convert_fusion.1
  1256.8 44.2 %reduce-scatter.20.cloned.1.call-done = bf16[512,288]{0,1:T(8,128)(2,1)} async-done(((bf16[512,2304]{0,1:T(8,128)(2,1)}), bf16[512,288]{0,1:T(8,128)(2,1)}) %reduce-scatter.20.cloned.1.call-update) | async-done | bytes 294928 | tf_op jit(solution)/shard_map/reduce_scatter | solution.py:244
  1302.8 38.1 %reduce-scatter.16.cloned.1.call-done = bf16[288,256]{1,0:T(8,128)(2,1)} async-done(((bf16[2304,256]{1,0:T(8,128)(2,1)}), bf16[288,256]{1,0:T(8,128)(2,1)}) %reduce-scatter.16.cloned.1.call-update) | async-done | bytes 147472 | tf_op jit(solution)/shard_map/reduce_scatter | solution.py:238
  1342.5 38.6 %reduce-scatter.18.cloned.1.call-done = bf16[288,256]{1,0:T(8,128)(2,1)} async-done(((bf16[2304,256]{1,0:T(8,128)(2,1)}), bf16[288,256]{1,0:T(8,128)(2,1)}) %reduce-scatter.18.cloned.1.call-update) | async-done | bytes 147472 | tf_op jit(solution)/shard_map/reduce_scatter | solution.py:241
  1382.8 96.9 %all-reduce.18.cloned.1.call-done = bf16[512,2304]{1,0:T(8,128)(2,1)} async-done(((bf16[512,2304]{1,0:T(8,128)(2,1)}), bf16[512,2304]{1,0:T(8,128)(2,1)}) %all-reduce.18.cloned.1.call-update) | async-done | bytes 2359312 | tf_op jit(solution)/shard_map/psum | solution.py:224
  1483.2 24.0 %all-reduce.8 = (bf16[2304]{0:T(1024)(128)(2,1)S(1)}, bf16[2304]{0:T(1024)(128)(2,1)S(1)}, bf16[2304]{0:T(1024)(128)(2,1)S(1)}, bf16[2304]{0:T(1024)(128)(2,1)S(1)}) all-reduce(bf16[2304]{0:T(1024)(128)(2,1)S(1)} %get-tuple-element.658, ...), channel_id=13, replica_groups=mesh['fsdp'=2,'ctx'=4,'tp'=4] {'fsdp','ctx'}, use_global_device_ids=true, to_apply=%region_29.30.clone | all-reduce | flops 9216 | bytes 36864
  1516.0 48.4 %reduce-scatter.26.cloned.1.call-done = bf16[2304,288]{0,1:T(8,128)(2,1)} async-done(((bf16[2304,2304]{0,1:T(8,128)(2,1)}), bf16[2304,288]{0,1:T(8,128)(2,1)}) %reduce-scatter.26.cloned.1.call-update) | async-done | bytes 1327120 | tf_op jit(solution)/shard_map/reduce_scatter | solution.py:259
  1567.4 82.8 %reduce-scatter.22.cloned.1.call-done = bf16[288,2304]{1,0:T(8,128)(2,1)} async-done(((bf16[2304,2304]{1,0:T(8,128)(2,1)}), bf16[288,2304]{1,0:T(8,128)(2,1)}) %reduce-scatter.22.cloned.1.call-update) | async-done | bytes 1327120 | tf_op jit(solution)/shard_map/reduce_scatter | solution.py:253
  1653.1 82.8 %reduce-scatter.24.cloned.1.call-done = bf16[288,2304]{1,0:T(8,128)(2,1)} async-done(((bf16[2304,2304]{1,0:T(8,128)(2,1)}), bf16[288,2304]{1,0:T(8,128)(2,1)}) %reduce-scatter.24.cloned.1.call-update) | async-done | bytes 1327120 | tf_op jit(solution)/shard_map/reduce_scatter | solution.py:256
  (339 shorter events, 211.3 us)
Async XLA Ops:
  7.2 36.0 %all-gather.15.cloned.1.call-start = ((), (), s32[]{:S(2)}) async-start(), calls=%async_computation.10 | async-start | bytes 1327104 | tf_op jit(solution)/shard_map/all_gather | solution.py:98
  7.9 55.0 %all-gather.17.cloned.1.call-start = ((), (), s32[]{:S(2)}) async-start(), calls=%async_computation.11 | async-start | bytes 1327104 | tf_op jit(solution)/shard_map/all_gather | solution.py:99
  8.7 73.2 %all-gather.29.cloned.1.call-start = ((), (), s32[]{:S(2)}) async-start(), calls=%async_computation.29 | async-start | bytes 1310720 | tf_op jit(solution)/shard_map/all_gather | solution.py:124
  40.0 76.8 %copy-start.35 = (f32[2304]{0:T(1024)}, f32[2304]{0:T(1024)S(1)}, u32[]{:S(2)}) copy-start(f32[2304]{0:T(1024)S(1)} %convert_element_type.212) | copy-start | bytes 27652
  40.8 25.6 %copy-start.49 = (f32[128]{0:T(128)}, f32[128]{0:T(128)S(1)}, u32[]{:S(2)}) copy-start(f32[128]{0:T(128)S(1)} %multiply_power_fusion) | copy-start | bytes 1540
  40.9 25.5 %copy-start.39 = (f32[512]{0:T(512)}, f32[512]{0:T(512)S(1)}, u32[]{:S(2)}) copy-start(f32[512]{0:T(512)S(1)} %get-tuple-element.717) | copy-start | bytes 6148
  43.1 73.8 %copy-start.46 = (f32[512]{0:T(512)}, f32[512]{0:T(512)S(1)}, u32[]{:S(2)}) copy-start(f32[512]{0:T(512)S(1)} %add_rsqrt_fusion.3) | copy-start | bytes 6148
  48.2 64.4 %all-gather.13.cloned.1.call-start = ((), (), s32[]{:S(2)}) async-start(), calls=%async_computation.9 | async-start | bytes 2654208 | tf_op jit(solution)/shard_map/all_gather | solution.py:97
  48.8 82.5 %all-gather.19.cloned.1.call-start = ((), (), s32[]{:S(2)}) async-start(), calls=%async_computation.12 | async-start | bytes 1310720 | tf_op jit(solution)/shard_map/all_gather | solution.py:125
  65.7 96.4 %all-gather.21.cloned.1.call-start = ((), (), s32[]{:S(2)}) async-start(), calls=%async_computation.13 | async-start | bytes 2654208 | tf_op jit(solution)/shard_map/all_gather | solution.py:100
  66.3 424.1 %all-gather.31.cloned.1.call-start = ((), (), s32[]{:S(2)}) async-start(), calls=%async_computation.30 | async-start | bytes 23592960 | tf_op jit(solution)/shard_map/all_gather | solution.py:148
  167.7 387.3 %all-gather.23.cloned.1.call-start = ((), (), s32[]{:S(2)}) async-start(), calls=%async_computation.14 | async-start | bytes 11943936 | tf_op jit(solution)/shard_map/all_gather | solution.py:152
  168.4 452.3 %all-gather.25.cloned.1.call-start = ((), (), s32[]{:S(2)}) async-start(), calls=%async_computation.15 | async-start | bytes 11943936 | tf_op jit(solution)/shard_map/all_gather | solution.py:153
  169.2 517.1 %all-gather.27.cloned.1.call-start = ((), (), s32[]{:S(2)}) async-start(), calls=%async_computation.16 | async-start | bytes 11943936 | tf_op jit(solution)/shard_map/all_gather | solution.py:154
  169.8 700.3 %all-reduce.14.cloned.1.call-start = ((), (), s32[]{:S(2)}) async-start(), calls=%async_computation.17 | async-start | bytes 9437184 | tf_op jit(solution)/shard_map/psum | solution.py:162
  508.4 112.3 %copy-start.19 = (bf16[512,2304]{1,0:T(8,128)(2,1)}, bf16[512,2304]{1,0:T(8,128)(2,1)S(1)}, u32[]{:S(2)}) copy-start(bf16[512,2304]{1,0:T(8,128)(2,1)S(1)} %multiply_convert_fusion.3) | copy-start | bytes 7077892
  697.9 175.0 %copy-start.11 = (bf16[1,512,2304]{2,1,0:T(8,128)(2,1)S(1)}, bf16[1,512,2304]{2,1,0:T(8,128)(2,1)}, u32[]{:S(2)}) copy-start(bf16[1,512,2304]{2,1,0:T(8,128)(2,1)} %param.33) | copy-start | bytes 7077892
  698.0 390.8 %all-reduce.16.cloned.1.call-start = ((), (), s32[]{:S(2)}) async-start(), calls=%async_computation.18 | async-start | bytes 9437184 | tf_op jit(solution)/shard_map/psum | solution.py:177
  917.6 256.9 %reduce-scatter.10.cloned.1.call-start = ((), (), s32[]{:S(2)}) async-start(), calls=%async_computation.19 | async-start | bytes 2621440 | tf_op jit(solution)/shard_map/reduce_scatter | solution.py:210
  1144.0 64.6 %reduce-scatter.12.cloned.1.call-start = ((), (), s32[]{:S(2)}) async-start(), calls=%async_computation.20 | async-start | bytes 2621440 | tf_op jit(solution)/shard_map/reduce_scatter | solution.py:211
  1144.6 110.3 %reduce-scatter.14.cloned.1.call-start = ((), (), s32[]{:S(2)}) async-start(), calls=%async_computation.22 | async-start | bytes 2654208 | tf_op jit(solution)/shard_map/reduce_scatter | solution.py:235
  1149.6 25.0 %copy-start.40 = (f32[512]{0:T(512)S(1)}, f32[512]{0:T(512)}, u32[]{:S(2)}) copy-start(f32[512]{0:T(512)} %copy-done.39) | copy-start | bytes 6148
  1149.6 151.4 %reduce-scatter.20.cloned.1.call-start = ((), (), s32[]{:S(2)}) async-start(), calls=%async_computation.25 | async-start | bytes 2654208 | tf_op jit(solution)/shard_map/reduce_scatter | solution.py:244
  1154.5 186.4 %reduce-scatter.16.cloned.1.call-start = ((), (), s32[]{:S(2)}) async-start(), calls=%async_computation.23 | async-start | bytes 1327104 | tf_op jit(solution)/shard_map/reduce_scatter | solution.py:238
  1179.0 202.1 %reduce-scatter.18.cloned.1.call-start = ((), (), s32[]{:S(2)}) async-start(), calls=%async_computation.24 | async-start | bytes 1327104 | tf_op jit(solution)/shard_map/reduce_scatter | solution.py:241
  1211.7 268.0 %all-reduce.18.cloned.1.call-start = ((), (), s32[]{:S(2)}) async-start(), calls=%async_computation.21 | async-start | bytes 4718592 | tf_op jit(solution)/shard_map/psum | solution.py:224
  1217.8 346.6 %reduce-scatter.26.cloned.1.call-start = ((), (), s32[]{:S(2)}) async-start(), calls=%async_computation.28 | async-start | bytes 11943936 | tf_op jit(solution)/shard_map/reduce_scatter | solution.py:259
  1228.4 421.8 %reduce-scatter.22.cloned.1.call-start = ((), (), s32[]{:S(2)}) async-start(), calls=%async_computation.26 | async-start | bytes 11943936 | tf_op jit(solution)/shard_map/reduce_scatter | solution.py:253
  1238.7 497.1 %reduce-scatter.24.cloned.1.call-start = ((), (), s32[]{:S(2)}) async-start(), calls=%async_computation.27 | async-start | bytes 11943936 | tf_op jit(solution)/shard_map/reduce_scatter | solution.py:256
  1249.5 233.7 %copy-start.43 = (bf16[2304]{0:T(1024)(128)(2,1)S(1)}, bf16[2304]{0:T(1024)(128)(2,1)}, u32[]{:S(2)}) copy-start(bf16[2304]{0:T(1024)(128)(2,1)} %get-tuple-element.654) | copy-start | bytes 13828
  1249.5 233.7 %copy-start.44 = (bf16[2304]{0:T(1024)(128)(2,1)S(1)}, bf16[2304]{0:T(1024)(128)(2,1)}, u32[]{:S(2)}) copy-start(bf16[2304]{0:T(1024)(128)(2,1)} %get-tuple-element.656) | copy-start | bytes 13828
  1249.5 233.7 %copy-start.45 = (bf16[2304]{0:T(1024)(128)(2,1)S(1)}, bf16[2304]{0:T(1024)(128)(2,1)}, u32[]{:S(2)}) copy-start(bf16[2304]{0:T(1024)(128)(2,1)} %get-tuple-element.652) | copy-start | bytes 13828
  (60 other events, 406.3 us)
Sparse Core Ops, SparseCore 0:
  9.9 26.9 all-gather.14
  38.7 24.1 all-gather.16
  65.0 16.7 all-gather.28
  83.6 28.9 all-gather.12
  114.6 16.7 all-gather.18
  133.1 29.0 all-gather.20
  167.7 322.5 all-gather.30
  492.3 62.6 all-gather.22
  556.8 63.8 all-gather.24
  622.4 63.8 all-gather.26
  698.1 171.9 all-reduce.13
  917.8 170.9 all-reduce.15
  1144.1 30.4 reduce-scatter.9
  1177.1 31.4 reduce-scatter.11
  1212.4 42.5 reduce-scatter.13
  1258.5 42.4 reduce-scatter.19
  1304.0 36.7 reduce-scatter.15
  1344.3 36.7 reduce-scatter.17
  1384.1 95.6 all-reduce.17
  1483.1 81.2 reduce-scatter.25
  1567.9 82.2 reduce-scatter.21
  1653.6 82.1 reduce-scatter.23
